TPU v7x, 512 devices: a whole 4x4x16 slice. The times are simulated.
512 devices in a mesh: lev: 4 (over y), tile: 64 (over z_lo, x, core), sec: 2 (over z_hi).
Axes of the slice: x: 4, y: 4, z: 16 (z_hi: 2, z_lo: 8; z = z_hi * 8 + z_lo), core: 2. Of those that a mesh axis runs over, the one named last changes fastest.
Arguments:
- fields: float32 [3, 64, 4, 128, 360], P(None, ('lev', 'sec'), None, 'tile'), may hold values from -6 to 6
- surface: float32 [4, 128, 360], P(None, 'tile'), may hold values from -6 to 6
- cot_fields: float32 [3, 64, 4, 128, 360], P(None, ('lev', 'sec'), None, 'tile'), may hold values from -6 to 6
- cot_surface: float32 [4, 128, 360], P(None, 'tile'), may hold values from -6 to 6
- land_sea: int32 [128, 360], P('tile'), may hold values 0 or 1
- w_in: bfloat16 [192, 384], replicated, may hold values from -0.4375 to 0.4375
- w_mid: bfloat16 [384, 384], replicated, may hold values from -0.3125 to 0.3125
- w_out: bfloat16 [384, 192], replicated, may hold values from -0.3125 to 0.3125
- bias_in: float32 [2, 384], replicated, may hold values from -4 to 4
Outputs:
- final_fields: float32 [3, 64, 4, 128, 360], P(None, ('lev', 'sec'), None, 'tile')
- final_surface: float32 [4, 128, 360], P(None, 'tile')
- fields_grad: float32 [3, 64, 4, 128, 360], P(None, ('lev', 'sec'), None, 'tile')
- surface_grad: float32 [4, 128, 360], P(None, 'tile')
- w_in_grad: float32 [192, 384], replicated
- w_mid_grad: float32 [384, 384], replicated
- w_out_grad: float32 [384, 192], replicated
- bias_grad: float32 [2, 384], replicated
Inputs may be any that keep to these rules, and one draw needn't show every extreme that they name: `land_sea`: 1 marks land, 0 sea.
All inputs are finite; a program needn't handle non-finite values. No bound on the sum of `land_sea` on one device may be relied on, other than what follows from the above.
Results may differ from a plain program's by a relative error of at most 0.005.
Values may be sent and summed in bfloat16 or wider, within the bound.
A program may use at most 64 MiB of HBM per device.

v0:
```python
import math
import jax
import jax.numpy as jnp
from jax import lax
from jax.sharding import PartitionSpec as P

NLEV = 64
STEPS = 2
TIME_STEP = 0.1
COS_FLOOR = 0.2
INV_SQRT_TWO = 1.0 / math.sqrt(2.0)
INV_SQRT_TWO_PI = 1.0 / math.sqrt(2.0 * math.pi)


def extended(value, sides, width):
    for axis, dim in sides:
        size, length = (lax.axis_size(axis), value.shape[dim])
        up = [(i, (i + 1) % size) for i in range(size - 1)]
        down = [(j, i) for i, j in up]
        last = lax.slice_in_dim(value, length - width, length, axis=dim)
        first = lax.slice_in_dim(value, 0, width, axis=dim)
        before = lax.ppermute(last, axis, up)
        after = lax.ppermute(first, axis, down)
        value = jnp.concatenate([before, value, after], axis=dim)
    return value


def carried_in(part, axis, combine, identity):
    place = lax.axis_index(axis)
    gathered = jax.tree.map(lambda a: lax.all_gather(a, axis), part)
    state = jax.tree.map(lambda a, e: jnp.zeros_like(a) + jnp.asarray(e, a.dtype), part, identity)

    def one(lap, state):
        return combine(
            state, jax.tree.map(lambda a: lax.dynamic_index_in_dim(a, lap, 0, False), gathered)
        )

    return lax.fori_loop(0, place, one, state)


def gelu_slope(values):
    cumulative = 0.5 * (1.0 + lax.erf(values * INV_SQRT_TWO))
    density = jnp.exp(-0.5 * values * values) * INV_SQRT_TWO_PI
    return cumulative + values * density


def lon_change(values, x_factor):
    return (jnp.roll(values, -1, axis=-1) - jnp.roll(values, 1, axis=-1)) * x_factor


def lat_change(values):
    padded = extended(values, (("tile", 2),), 1)
    return (padded[:, :, 2:, :] - padded[:, :, :-2, :]) * 0.5


def add_pairs(earlier, later):
    return (earlier[0] + later[0], earlier[1] + later[1])


def vertical_sums(rising_in, falling_in):
    rising_run = jnp.cumsum(rising_in, axis=0)
    falling_run = jnp.flip(jnp.cumsum(jnp.flip(falling_in, 0), axis=0), 0)
    rising_part = rising_run[-1]
    falling_part = falling_run[0]
    zeros_part = jnp.zeros_like(rising_part)
    before, falling_before = carried_in(
        (rising_part, falling_part), ("lev", "sec"), add_pairs, (zeros_part, zeros_part)
    )
    column_sum, falling_total = lax.psum((rising_part, falling_part), ("lev", "sec"))
    beyond = falling_total - falling_before - falling_part
    return (before + rising_run, beyond + falling_run, column_sum)


def on_device(fields, surface, cot_fields, cot_surface, land_sea, w_in, w_mid, w_out, bias_in):
    lev_dev = fields.shape[1]
    batch_size = fields.shape[2]
    lat_dev = fields.shape[3]
    lon_cells = fields.shape[4]
    level_shape = fields.shape
    shard_count = lax.axis_size(("lev", "sec"))
    position = lax.axis_index(("lev", "sec"))
    lat_total = lat_dev * lax.axis_size("tile")
    row_ids = (lax.axis_index("tile") * lat_dev + jnp.arange(lat_dev)).astype(jnp.float32)
    latitude = -0.5 * math.pi + (row_ids + 0.5) * (math.pi / lat_total)
    x_factor = (0.5 / jnp.maximum(jnp.cos(latitude), COS_FLOOR))[:, None]
    sin_lat = jnp.sin(latitude)[:, None]
    level_ids = (position * lev_dev + jnp.arange(lev_dev)).astype(jnp.float32)
    layer_thickness_fraction = (1.0 / (level_ids + 1.0))[:, None, None, None]
    col_count = batch_size * lat_dev * lon_cells // shard_count
    mask_all = jnp.broadcast_to(land_sea[None], (batch_size, lat_dev, lon_cells)).reshape(-1)
    mask_cols = lax.dynamic_slice_in_dim(mask_all, position * col_count, col_count)
    land_cols = (mask_cols > 0)[None, :]
    bias_cols = jnp.where(mask_cols[None, :] > 0, bias_in[1][:, None], bias_in[0][:, None])

    def to_columns(values):
        flattened = values.reshape(values.shape[0], values.shape[1], -1)
        arrived = lax.all_to_all(flattened, ("lev", "sec"), split_axis=2, concat_axis=1, tiled=True)
        return arrived.reshape(arrived.shape[0] * arrived.shape[1], arrived.shape[2])

    def to_levels(values):
        regrouped = values.reshape(level_shape[0], -1, values.shape[1])
        arrived = lax.all_to_all(regrouped, ("lev", "sec"), split_axis=1, concat_axis=2, tiled=True)
        return arrived.reshape(level_shape)

    current_fields_bundle, current_ground_pressure = (fields, surface)
    stored = []
    for instant in range(STEPS):
        x_cols = to_columns(current_fields_bundle.astype(jnp.bfloat16))
        first_pre = (
            jnp.einsum("fh,fc->hc", w_in, x_cols, preferred_element_type=jnp.float32) + bias_cols
        )
        first_act = jax.nn.gelu(first_pre, approximate=False).astype(jnp.bfloat16)
        second_pre = jnp.einsum("io,ic->oc", w_mid, first_act, preferred_element_type=jnp.float32)
        second_act = jax.nn.gelu(second_pre, approximate=False).astype(jnp.bfloat16)
        first_pre, first_act, second_pre, second_act = (
            first_pre,
            first_act,
            second_pre,
            second_act,
        )
        tendency = jnp.einsum(
            "hf,hc->fc", w_out, second_act, preferred_element_type=jnp.float32
        ).astype(jnp.bfloat16)
        zonal_velocity = current_fields_bundle[0]
        meridional_velocity = current_fields_bundle[1]
        thermal_field = current_fields_bundle[2]
        velocity_spreading = lon_change(zonal_velocity, x_factor) + lat_change(meridional_velocity)
        dynamics_prefix, dynamics_suffix, dynamics_column_sum = vertical_sums(
            velocity_spreading, layer_thickness_fraction * thermal_field
        )
        gravity_potential_elevation = dynamics_suffix + current_ground_pressure[None]
        zonal_tend = (
            -lon_change(gravity_potential_elevation, x_factor) + sin_lat * meridional_velocity
        )
        merid_tend = -lat_change(gravity_potential_elevation) - sin_lat * zonal_velocity
        temp_tend = -(dynamics_prefix / NLEV)
        dyn_fields = jnp.stack([zonal_tend, merid_tend, temp_tend])
        dyn_surface = -dynamics_column_sum / NLEV
        physics = to_levels(tendency).astype(jnp.float32)
        current_fields_bundle = current_fields_bundle + TIME_STEP * (dyn_fields + physics)
        current_ground_pressure = current_ground_pressure + TIME_STEP * dyn_surface
        stored.append((x_cols, first_pre, first_act, second_pre, second_act))
    field_bar, surface_bar = (cot_fields, cot_surface)
    gradient = (
        jnp.zeros(w_in.shape, jnp.float32),
        jnp.zeros(w_mid.shape, jnp.float32),
        jnp.zeros(w_out.shape, jnp.float32),
        jnp.zeros(bias_in.shape, jnp.float32),
    )
    for instant in reversed(range(STEPS)):
        x_cols, first_pre, first_act, second_pre, second_act = stored[instant]
        tend_bar = to_columns((TIME_STEP * field_bar).astype(jnp.bfloat16))
        second_bar = (
            jnp.einsum("hf,fc->hc", w_out, tend_bar, preferred_element_type=jnp.float32)
            * gelu_slope(second_pre)
        ).astype(jnp.bfloat16)
        first_bar = (
            jnp.einsum("io,oc->ic", w_mid, second_bar, preferred_element_type=jnp.float32)
            * gelu_slope(first_pre)
        ).astype(jnp.bfloat16)
        input_bar = jnp.einsum(
            "fh,hc->fc", w_in, first_bar, preferred_element_type=jnp.float32
        ).astype(jnp.bfloat16)
        first_wide = first_bar.astype(jnp.float32)
        zero_f = jnp.zeros((), jnp.float32)
        sea_part = jnp.sum(jnp.where(land_cols, zero_f, first_wide), axis=1)
        land_part = jnp.sum(jnp.where(land_cols, first_wide, zero_f), axis=1)
        local_grads = (
            jnp.einsum("fc,hc->fh", x_cols, first_bar, preferred_element_type=jnp.float32),
            jnp.einsum("ic,oc->io", first_act, second_bar, preferred_element_type=jnp.float32),
            jnp.einsum("hc,fc->hf", second_act, tend_bar, preferred_element_type=jnp.float32),
            jnp.stack([sea_part, land_part]),
        )
        a_zonal = field_bar[0]
        a_merid = field_bar[1]
        a_temp = field_bar[2]
        height_bar = lon_change(a_zonal, x_factor) + lat_change(a_merid)
        prefix, suffix, column_sum = vertical_sums(height_bar, a_temp)
        temp_bar = layer_thickness_fraction * prefix
        div_bar = (-suffix - surface_bar[None]) / NLEV
        zonal_bar = -lon_change(div_bar, x_factor) - sin_lat * a_merid
        merid_bar = -lat_change(div_bar) + sin_lat * a_zonal
        adj_fields = jnp.stack([zonal_bar, merid_bar, temp_bar])
        input_levels = to_levels(input_bar).astype(jnp.float32)
        field_bar = field_bar + TIME_STEP * adj_fields + input_levels
        surface_bar = surface_bar + TIME_STEP * column_sum
        summed = lax.psum(
            (local_grads[0], local_grads[1], local_grads[2], local_grads[3]), ("lev", "tile", "sec")
        )
        gradient = jax.tree.map(jnp.add, gradient, summed)
    return (
        current_fields_bundle,
        current_ground_pressure,
        field_bar,
        surface_bar,
        gradient[0],
        gradient[1],
        gradient[2],
        gradient[3],
    )


def solution(mesh):
    return jax.shard_map(
        on_device,
        mesh=mesh,
        in_specs=(
            P(None, ("lev", "sec"), None, "tile", None),
            P(None, "tile", None),
            P(None, ("lev", "sec"), None, "tile", None),
            P(None, "tile", None),
            P("tile", None),
            P(),
            P(),
            P(),
            P(),
        ),
        out_specs=(
            P(None, ("lev", "sec"), None, "tile", None),
            P(None, "tile", None),
            P(None, ("lev", "sec"), None, "tile", None),
            P(None, "tile", None),
            P(),
            P(),
            P(),
            P(),
        ),
        check_vma=False,
    )
```

profile of v0, /device:TPU:8, one launch (start us, length us, event | category | flops | bytes accessed | tf_op | source)
XLA Modules:
  0.0 1526.2 jit_solution(4728833632779786206)
XLA Ops:
  11.7 3.6 collective-permute-start.1
  19.7 3.7 collective-permute-start.9
  25.1 4.8 copy.305
  30.0 2.8 reshape.435
  32.7 18.2 %all-to-all-start = ((bf16[8,2,4320]{2,1,0:T(2,128)(2,1)}), bf16[8,2,4320]{2,1,0:T(2,128)(2,1)}, u32[]{:S(2)}, u32[]{:S(2)}) async-start(bf16[8,2,4320]{2,1,0:T(2,128)(2,1)} %reshape.435), calls=%async_computation | async-start | bytes 278528 | tf_op jit(solution)/shard_map/all_to_all | solution.py:97
  62.3 63.0 %all_gather.29 = f32[8,4,2,360]{3,1,2,0:T(4,128)} all-gather(f32[1,4,2,360]{3,1,2,0:T(4,128)S(1)} %copy.336), channel_id=1, replica_groups=mesh['lev'=4,'tile'=64,'sec'=2] {'lev','sec'}, dimensions={0}, use_global_device_ids=true | all-gather | bytes 103680 | tf_op jit(solution)/shard_map/all_gather | solution.py:30
  125.9 78.4 %all-reduce.2 = (f32[4,2,360]{2,1,0:T(2,128)}, f32[4,2,360]{2,1,0:T(2,128)}) all-reduce(f32[4,2,360]{2,1,0:T(2,128)S(1)} %get-tuple-element.428, f32[4,2,360]{2,1,0:T(2,128)S(1)} %get-tuple-element.453), channel_id=1, replica_groups=mesh['lev'=4,'tile'=64,'sec'=2] {'lev','sec'}, use_global_device_ids=true, to_apply=%region_1.2 | all-reduce | flops 5760 | bytes 46080 | tf_op jit(solution)/shard_map/psum | solution.py:69
  204.3 2.7 copy.380
  207.0 2.8 reshape.439
  209.8 63.3 %all_gather.25 = f32[8,4,2,360]{3,1,2,0:T(4,128)S(1)} all-gather(f32[1,4,2,360]{3,1,2,0:T(4,128)S(1)} %copy.295), channel_id=1, replica_groups=mesh['lev'=4,'tile'=64,'sec'=2] {'lev','sec'}, dimensions={0}, use_global_device_ids=true | all-gather | bytes 103680 | tf_op jit(solution)/shard_map/all_gather | solution.py:30
  275.2 63.2 %all_gather.24 = f32[8,4,2,360]{3,1,2,0:T(4,128)S(1)} all-gather(f32[1,4,2,360]{3,1,2,0:T(4,128)S(1)} %copy.294), channel_id=1, replica_groups=mesh['lev'=4,'tile'=64,'sec'=2] {'lev','sec'}, dimensions={0}, use_global_device_ids=true | all-gather | bytes 103680 | tf_op jit(solution)/shard_map/all_gather | solution.py:30
  343.8 62.9 %all_gather.28 = f32[8,4,2,360]{3,1,2,0:T(4,128)S(1)} all-gather(f32[1,4,2,360]{3,1,2,0:T(4,128)S(1)} %copy.335), channel_id=1, replica_groups=mesh['lev'=4,'tile'=64,'sec'=2] {'lev','sec'}, dimensions={0}, use_global_device_ids=true | all-gather | bytes 103680 | tf_op jit(solution)/shard_map/all_gather | solution.py:30
  411.7 3.6 collective-permute-start.3
  417.2 3.6 collective-permute-start.11
  422.9 8.4 all-to-all-start.4
  431.4 3.0 reshape.436
  434.4 2.2 copy.376
  436.6 3.2 fusion.23
  443.1 2.4 all-to-all-done.4
  445.5 12.0 all-to-all-start.1
  461.8 3.0 reshape.440
  464.8 2.2 copy.382
  467.1 10.0 all-to-all-done.1
  484.4 3.0 collective-permute-start.5
  488.0 2.7 copy.377
  490.7 2.8 reshape.437
  493.5 4.5 all-to-all-start.2
  497.9 62.6 %all_gather.27 = f32[8,4,2,360]{3,1,2,0:T(4,128)S(1)} all-gather(f32[1,4,2,360]{3,1,2,0:T(4,128)S(1)} %copy.318), channel_id=1, replica_groups=mesh['lev'=4,'tile'=64,'sec'=2] {'lev','sec'}, dimensions={0}, use_global_device_ids=true | all-gather | bytes 103680 | tf_op jit(solution)/shard_map/all_gather | solution.py:30
  563.1 63.3 %all_gather.26 = f32[8,4,2,360]{3,1,2,0:T(4,128)S(1)} all-gather(f32[1,4,2,360]{3,1,2,0:T(4,128)S(1)} %copy.317), channel_id=1, replica_groups=mesh['lev'=4,'tile'=64,'sec'=2] {'lev','sec'}, dimensions={0}, use_global_device_ids=true | all-gather | bytes 103680 | tf_op jit(solution)/shard_map/all_gather | solution.py:30
  627.4 3.0 reshape.438
  638.0 14.9 all-to-all-start.5
  656.1 10.7 all-to-all-done.5
  666.8 5.6 all-to-all-start.3
  677.4 3.6 collective-permute-start.13
  681.1 2.7 copy.383
  683.8 2.8 reshape.441
  688.7 14.6 all-to-all-start.6
  704.9 62.2 %all_gather.31 = f32[8,4,2,360]{3,1,2,0:T(4,128)S(1)} all-gather(f32[1,4,2,360]{3,1,2,0:T(4,128)S(1)} %copy.357), channel_id=1, replica_groups=mesh['lev'=4,'tile'=64,'sec'=2] {'lev','sec'}, dimensions={0}, use_global_device_ids=true | all-gather | bytes 103680 | tf_op jit(solution)/shard_map/all_gather | solution.py:30
  769.2 63.2 %all_gather.30 = f32[8,4,2,360]{3,1,2,0:T(4,128)S(1)} all-gather(f32[1,4,2,360]{3,1,2,0:T(4,128)S(1)} %copy.356), channel_id=1, replica_groups=mesh['lev'=4,'tile'=64,'sec'=2] {'lev','sec'}, dimensions={0}, use_global_device_ids=true | all-gather | bytes 103680 | tf_op jit(solution)/shard_map/all_gather | solution.py:30
  833.4 160.5 %all-reduce.8.cloned.1.call-done = (f32[4,2,360]{2,1,0:T(2,128)}, f32[4,2,360]{2,1,0:T(2,128)}, f32[4,2,360]{2,1,0:T(2,128)}, f32[4,2,360]{2,1,0:T(2,128)}, f32[4,2,360]{2,1,0:T(2,128)}, /*index=5*/f32[4,2,360]{2,1,0:T(2,128)}) async-done(((f32[4,2,360]{2,1,0:T(2,128)}, f32[4,2,360]{2,1,0:T(2,128)}, f32[4,2,360]{2,1,0:T(2,128)}, f32[4,2,360]{2,1,0:T(2,128)}, f32[4,2,360]{2,1,0:T(2,128)}, ...) | async-done | bytes 69136 | tf_op jit(solution)/shard_map/psum | solution.py:69
  1001.3 3.0 collective-permute-start.15
  1005.6 3.5 collective-permute-start.7
  1012.4 3.0 reshape.442
  1015.4 2.2 copy.385
  1023.6 4.7 all-to-all-start.7
  1029.3 2.1 convolution_add_fusion
  1031.5 112.3 %psum.131 = f32[2,384]{1,0:T(2,128)} all-reduce(f32[2,384]{1,0:T(2,128)S(1)} %maximum_add_fusion.2), channel_id=1, replica_groups=mesh['lev'=4,'tile'=64,'sec'=2] {'lev','tile','sec'}, use_global_device_ids=true, to_apply=%region_32.33 | all-reduce | flops 768 | bytes 6144 | tf_op jit(solution)/shard_map/psum | solution.py:187
  1144.8 368.7 %all-reduce.6.cloned.1.call-done = (f32[192,384]{1,0:T(8,128)}, f32[384,384]{1,0:T(8,128)}, f32[384,192]{0,1:T(8,128)}) async-done(((f32[192,384]{1,0:T(8,128)}, f32[384,384]{1,0:T(8,128)}, f32[384,192]{0,1:T(8,128)}), (f32[192,384]{1,0:T(8,128)}, f32[384,384]{1,0:T(8,128)}, f32[384,192]{0,1:T(8,128)})) %all-reduce.6.cloned.1.call-update) | async-done | bytes 1179664 | tf_op jit(solution)/shard_map/psum | solution.py:187
  (371 shorter events, 105.7 us)
Async XLA Ops:
  8.0 431.8 %copy-start = (bf16[384,384]{1,0:T(8,128)(2,1)S(1)}, bf16[384,384]{1,0:T(8,128)(2,1)}, u32[]{:S(2)}) copy-start(bf16[384,384]{1,0:T(8,128)(2,1)} %param.23) | copy-start | bytes 884740
  10.4 262.7 %collective-permute-start = (f32[8,4,1,360]{3,2,1,0:T(1,128)}, f32[8,4,1,360]{3,2,1,0:T(1,128)}, u32[]{:S(2)}, u32[]{:S(2)}) collective-permute-start(f32[8,4,1,360]{3,2,1,0:T(1,128)} %get-tuple-element.434), channel_id=1, source_target_pairs={{2,0},{4,2},{6,4},{8,6},{10,8},{12,10},{14,12},{16,14},{18,16},{20... | collective-permute-start | bytes 138248 | tf_op jit(solution)/shard_map/ppermute | solution.py:23
  11.7 261.4 %collective-permute-start.1 = (f32[8,4,1,360]{3,2,1,0:T(1,128)}, f32[8,4,1,360]{3,2,1,0:T(1,128)}, u32[]{:S(2)}, u32[]{:S(2)}) collective-permute-start(f32[8,4,1,360]{3,2,1,0:T(1,128)} %get-tuple-element.435), channel_id=1, source_target_pairs={{0,2},{2,4},{4,6},{6,8},{8,10},{10,12},{12,14},{14,16},{16,18},{18... | collective-permute-start | bytes 138248 | tf_op jit(solution)/shard_map/ppermute | solution.py:22
  18.4 323.5 %collective-permute-start.8 = (f32[8,4,1,360]{3,2,1,0:T(1,128)}, f32[8,4,1,360]{3,2,1,0:T(1,128)}, u32[]{:S(2)}, u32[]{:S(2)}) collective-permute-start(f32[8,4,1,360]{3,2,1,0:T(1,128)} %get-tuple-element.408), channel_id=1, source_target_pairs={{2,0},{4,2},{6,4},{8,6},{10,8},{12,10},{14,12},{16,14},{18,16},{20... | collective-permute-start | bytes 138248 | tf_op jit(solution)/shard_map/ppermute | solution.py:23
  19.7 322.2 %collective-permute-start.9 = (f32[8,4,1,360]{3,2,1,0:T(1,128)}, f32[8,4,1,360]{3,2,1,0:T(1,128)}, u32[]{:S(2)}, u32[]{:S(2)}) collective-permute-start(f32[8,4,1,360]{3,2,1,0:T(1,128)} %get-tuple-element.409), channel_id=1, source_target_pairs={{0,2},{2,4},{4,6},{6,8},{8,10},{10,12},{12,14},{14,16},{16,18},{18... | collective-permute-start | bytes 138248 | tf_op jit(solution)/shard_map/ppermute | solution.py:22
  32.7 390.2 %all-to-all-start = ((bf16[8,2,4320]{2,1,0:T(2,128)(2,1)}), bf16[8,2,4320]{2,1,0:T(2,128)(2,1)}, u32[]{:S(2)}, u32[]{:S(2)}) async-start(bf16[8,2,4320]{2,1,0:T(2,128)(2,1)} %reshape.435), calls=%async_computation | async-start | bytes 278528 | tf_op jit(solution)/shard_map/all_to_all | solution.py:97
  60.6 143.6 %copy-start.40 = (f32[8,4,2,360]{3,2,1,0:T(2,128)}, f32[8,4,2,360]{3,2,1,0:T(2,128)S(1)}, u32[]{:S(2)}) copy-start(f32[8,4,2,360]{3,2,1,0:T(2,128)S(1)} %fusion.183) | copy-start | bytes 276484
  209.7 132.2 %copy-start.20 = (f32[8,4,2,360]{3,2,1,0:T(2,128)S(1)}, f32[8,4,2,360]{3,2,1,0:T(2,128)}, u32[]{:S(2)}) copy-start(f32[8,4,2,360]{3,2,1,0:T(2,128)} %copy-done.19) | copy-start | bytes 276484
  209.8 132.2 %copy-start.43 = (f32[8,4,2,359]{3,2,1,0:T(2,128)S(1)}, f32[8,4,2,359]{3,2,1,0:T(2,128)}, u32[]{:S(2)}) copy-start(f32[8,4,2,359]{3,2,1,0:T(2,128)} %get-tuple-element.406) | copy-start | bytes 275716
  209.8 132.2 %copy-start.44 = (f32[8,4,2,359]{3,2,1,0:T(2,128)S(1)}, f32[8,4,2,359]{3,2,1,0:T(2,128)}, u32[]{:S(2)}) copy-start(f32[8,4,2,359]{3,2,1,0:T(2,128)} %get-tuple-element.407) | copy-start | bytes 275716
  209.8 132.2 %copy-start.54 = (f32[8,4,2,1]{3,2,1,0:T(2,128)S(1)}, f32[8,4,2,1]{3,2,1,0:T(2,128)}, u32[]{:S(2)}) copy-start(f32[8,4,2,1]{3,2,1,0:T(2,128)} %get-tuple-element.404) | copy-start | bytes 772
  209.8 132.2 %copy-start.55 = (f32[8,4,2,1]{3,2,1,0:T(2,128)S(1)}, f32[8,4,2,1]{3,2,1,0:T(2,128)}, u32[]{:S(2)}) copy-start(f32[8,4,2,1]{3,2,1,0:T(2,128)} %get-tuple-element.405) | copy-start | bytes 772
  209.8 198.5 %copy-start.65 = (f32[8]{0:T(128)S(1)}, f32[8]{0:T(128)}, u32[]{:S(2)}) copy-start(f32[8]{0:T(128)} %copy-done.64) | copy-start | bytes 100
  209.8 199.2 %copy-start.39 = (f32[8,4,2,360]{3,2,1,0:T(2,128)S(1)}, f32[8,4,2,360]{3,2,1,0:T(2,128)}, u32[]{:S(2)}) copy-start(f32[8,4,2,360]{3,2,1,0:T(2,128)} %copy-done.38) | copy-start | bytes 276484
  209.8 199.2 %copy-start.63 = (f32[4,2,360]{2,1,0:T(2,128)S(1)}, f32[4,2,360]{2,1,0:T(2,128)}, u32[]{:S(2)}) copy-start(f32[4,2,360]{2,1,0:T(2,128)} %get-tuple-element.346) | copy-start | bytes 34564
  209.8 199.2 %copy-start.58 = (f32[4,2,360]{2,1,0:T(2,128)S(1)}, f32[4,2,360]{2,1,0:T(2,128)}, u32[]{:S(2)}) copy-start(f32[4,2,360]{2,1,0:T(2,128)} %param.20) | copy-start | bytes 34564
  273.1 147.9 %copy-start.61 = (f32[2]{0:T(128)S(1)}, f32[2]{0:T(128)}, u32[]{:S(2)}) copy-start(f32[2]{0:T(128)} %fusion.149) | copy-start | bytes 28
  410.4 48.5 %collective-permute-start.2 = (f32[8,4,1,360]{3,2,1,0:T(1,128)}, f32[8,4,1,360]{3,2,1,0:T(1,128)}, u32[]{:S(2)}, u32[]{:S(2)}) collective-permute-start(f32[8,4,1,360]{3,2,1,0:T(1,128)} %get-tuple-element.426), channel_id=1, source_target_pairs={{2,0},{4,2},{6,4},{8,6},{10,8},{12,10},{14,12},{16,14},{18,16},{20... | collective-permute-start | bytes 138248 | tf_op jit(solution)/shard_map/ppermute | solution.py:23
  411.7 47.2 %collective-permute-start.3 = (f32[8,4,1,360]{3,2,1,0:T(1,128)}, f32[8,4,1,360]{3,2,1,0:T(1,128)}, u32[]{:S(2)}, u32[]{:S(2)}) collective-permute-start(f32[8,4,1,360]{3,2,1,0:T(1,128)} %get-tuple-element.427), channel_id=1, source_target_pairs={{0,2},{2,4},{4,6},{6,8},{8,10},{10,12},{12,14},{14,16},{16,18},{18... | collective-permute-start | bytes 138248 | tf_op jit(solution)/shard_map/ppermute | solution.py:22
  415.9 43.0 %collective-permute-start.10 = (f32[8,4,1,360]{3,2,1,0:T(1,128)}, f32[8,4,1,360]{3,2,1,0:T(1,128)}, u32[]{:S(2)}, u32[]{:S(2)}) collective-permute-start(f32[8,4,1,360]{3,2,1,0:T(1,128)} %get-tuple-element.398), channel_id=1, source_target_pairs={{2,0},{4,2},{6,4},{8,6},{10,8},{12,10},{14,12},{16,14},{18,16},{20... | collective-permute-start | bytes 138248 | tf_op jit(solution)/shard_map/ppermute | solution.py:23
  417.2 41.7 %collective-permute-start.11 = (f32[8,4,1,360]{3,2,1,0:T(1,128)}, f32[8,4,1,360]{3,2,1,0:T(1,128)}, u32[]{:S(2)}, u32[]{:S(2)}) collective-permute-start(f32[8,4,1,360]{3,2,1,0:T(1,128)} %get-tuple-element.399), channel_id=1, source_target_pairs={{0,2},{2,4},{4,6},{6,8},{8,10},{10,12},{12,14},{14,16},{16,18},{18... | collective-permute-start | bytes 138248 | tf_op jit(solution)/shard_map/ppermute | solution.py:22
  422.9 22.5 %all-to-all-start.4 = ((bf16[8,2,4320]{2,1,0:T(2,128)(2,1)}), bf16[8,2,4320]{2,1,0:T(2,128)(2,1)}, u32[]{:S(2)}, u32[]{:S(2)}) async-start(bf16[8,2,4320]{2,1,0:T(2,128)(2,1)} %reshape.439), calls=%async_computation.4 | async-start | bytes 278528 | tf_op jit(solution)/shard_map/all_to_all | solution.py:97
  445.5 31.6 %all-to-all-start.1 = ((bf16[3,64,360]{2,0,1:T(4,128)(2,1)}), bf16[3,64,360]{2,0,1:T(4,128)(2,1)}, u32[]{:S(2)}, u32[]{:S(2)}) async-start(bf16[3,64,360]{2,0,1:T(4,128)(2,1)} %copy.308), calls=%async_computation.1 | async-start | bytes 393216 | tf_op jit(solution)/shard_map/all_to_all | solution.py:102
  483.1 77.5 %collective-permute-start.4 = (f32[8,4,1,360]{3,2,1,0:T(1,128)}, f32[8,4,1,360]{3,2,1,0:T(1,128)S(1)}, u32[]{:S(2)}, u32[]{:S(2)}) collective-permute-start(f32[8,4,1,360]{3,2,1,0:T(1,128)} %get-tuple-element.420), channel_id=1, source_target_pairs={{2,0},{4,2},{6,4},{8,6},{10,8},{12,10},{14,12},{16,14},{18,16},{20... | collective-permute-start | bytes 138248 | tf_op jit(solution)/shard_map/ppermute | solution.py:23
  484.4 76.2 %collective-permute-start.5 = (f32[8,4,1,360]{3,2,1,0:T(1,128)}, f32[8,4,1,360]{3,2,1,0:T(1,128)S(1)}, u32[]{:S(2)}, u32[]{:S(2)}) collective-permute-start(f32[8,4,1,360]{3,2,1,0:T(1,128)} %get-tuple-element.421), channel_id=1, source_target_pairs={{0,2},{2,4},{4,6},{6,8},{8,10},{10,12},{12,14},{14,16},{16,18},{18... | collective-permute-start | bytes 138248 | tf_op jit(solution)/shard_map/ppermute | solution.py:22
  493.5 133.9 %all-to-all-start.2 = ((bf16[8,2,4320]{2,1,0:T(2,128)(2,1)}), bf16[8,2,4320]{2,1,0:T(2,128)(2,1)}, u32[]{:S(2)}, u32[]{:S(2)}) async-start(bf16[8,2,4320]{2,1,0:T(2,128)(2,1)} %reshape.437), calls=%async_computation.2 | async-start | bytes 278528 | tf_op jit(solution)/shard_map/all_to_all | solution.py:97
  638.0 28.9 %all-to-all-start.5 = ((bf16[3,64,360]{2,0,1:T(4,128)(2,1)}), bf16[3,64,360]{2,0,1:T(4,128)(2,1)S(1)}, u32[]{:S(2)}, u32[]{:S(2)}) async-start(bf16[3,64,360]{2,0,1:T(4,128)(2,1)} %copy.349), calls=%async_computation.5 | async-start | bytes 393216 | tf_op jit(solution)/shard_map/all_to_all | solution.py:102
  666.8 21.9 %all-to-all-start.3 = ((bf16[3,64,360]{2,0,1:T(4,128)(2,1)}), bf16[3,64,360]{2,0,1:T(4,128)(2,1)}, u32[]{:S(2)}, u32[]{:S(2)}) async-start(bf16[3,64,360]{2,0,1:T(4,128)(2,1)} %copy.333), calls=%async_computation.3 | async-start | bytes 393216 | tf_op jit(solution)/shard_map/all_to_all | solution.py:102
  676.2 91.0 %collective-permute-start.12 = (f32[8,4,1,360]{3,2,1,0:T(1,128)}, f32[8,4,1,360]{3,2,1,0:T(1,128)}, u32[]{:S(2)}, u32[]{:S(2)}) collective-permute-start(f32[8,4,1,360]{3,2,1,0:T(1,128)} %get-tuple-element.392), channel_id=1, source_target_pairs={{2,0},{4,2},{6,4},{8,6},{10,8},{12,10},{14,12},{16,14},{18,16},{20... | collective-permute-start | bytes 138248 | tf_op jit(solution)/shard_map/ppermute | solution.py:23
  677.4 89.7 %collective-permute-start.13 = (f32[8,4,1,360]{3,2,1,0:T(1,128)}, f32[8,4,1,360]{3,2,1,0:T(1,128)}, u32[]{:S(2)}, u32[]{:S(2)}) collective-permute-start(f32[8,4,1,360]{3,2,1,0:T(1,128)} %get-tuple-element.393), channel_id=1, source_target_pairs={{0,2},{2,4},{4,6},{6,8},{8,10},{10,12},{12,14},{14,16},{16,18},{18... | collective-permute-start | bytes 138248 | tf_op jit(solution)/shard_map/ppermute | solution.py:22
  686.6 146.1 %copy-start.67 = (f32[8]{0:T(128)S(1)}, f32[8]{0:T(128)}, u32[]{:S(2)}) copy-start(f32[8]{0:T(128)} %copy-done.64) | copy-start | bytes 100
  686.6 307.4 %copy-start.59 = (f32[4,2,360]{2,1,0:T(2,128)S(1)}, f32[4,2,360]{2,1,0:T(2,128)}, u32[]{:S(2)}) copy-start(f32[4,2,360]{2,1,0:T(2,128)} %param.20) | copy-start | bytes 34564
  686.6 309.7 %copy-start.37 = (f32[8,4,2,360]{3,2,1,0:T(2,128)S(1)}, f32[8,4,2,360]{3,2,1,0:T(2,128)}, u32[]{:S(2)}) copy-start(f32[8,4,2,360]{3,2,1,0:T(2,128)} %copy-done.36) | copy-start | bytes 276484
  686.6 310.4 %copy-start.60 = (f32[4,2,360]{2,1,0:T(2,128)S(1)}, f32[4,2,360]{2,1,0:T(2,128)}, u32[]{:S(2)}) copy-start(f32[4,2,360]{2,1,0:T(2,128)} %param.18) | copy-start | bytes 34564
  688.7 320.5 %copy-start.18 = (f32[1,8,4,2,360]{4,1,3,2,0:T(8,128)S(1)}, f32[1,8,4,2,360]{4,1,3,2,0:T(8,128)}, u32[]{:S(2)}) copy-start(f32[1,8,4,2,360]{4,1,3,2,0:T(8,128)} %copy-done.17) | copy-start | bytes 276484
  688.7 320.5 %copy-start.62 = (f32[2]{0:T(128)S(1)}, f32[2]{0:T(128)}, u32[]{:S(2)}) copy-start(f32[2]{0:T(128)} %fusion.149) | copy-start | bytes 28
  688.7 323.7 %all-to-all-start.6 = ((bf16[8,2,4320]{2,1,0:T(2,128)(2,1)}), bf16[8,2,4320]{2,1,0:T(2,128)(2,1)}, u32[]{:S(2)}, u32[]{:S(2)}) async-start(bf16[8,2,4320]{2,1,0:T(2,128)(2,1)} %reshape.441), calls=%async_computation.6 | async-start | bytes 278528 | tf_op jit(solution)/shard_map/all_to_all | solution.py:97
  703.3 290.7 %all-reduce.8.cloned.1.call-start = ((), (), s32[]{:S(2)}) async-start(), calls=%async_computation.9 | async-start | bytes 147456 | tf_op jit(solution)/shard_map/psum | solution.py:69
  704.2 305.3 %copy-start.4 = (f32[3,8,4,2,360]{4,1,3,2,0:T(8,128)S(1)}, f32[3,8,4,2,360]{4,1,3,2,0:T(8,128)}, u32[]{:S(2)}) copy-start(f32[3,8,4,2,360]{4,1,3,2,0:T(8,128)} %copy-done.3) | copy-start | bytes 829444
  767.1 243.2 %copy-start.24 = (f32[1,8,4,2,360]{4,1,3,2,0:T(8,128)S(1)}, f32[1,8,4,2,360]{4,1,3,2,0:T(8,128)}, u32[]{:S(2)}) copy-start(f32[1,8,4,2,360]{4,1,3,2,0:T(8,128)} %copy-done.23) | copy-start | bytes 276484
  767.1 243.2 %copy-start.26 = (f32[1,8,4,2,360]{4,1,3,2,0:T(8,128)S(1)}, f32[1,8,4,2,360]{4,1,3,2,0:T(8,128)}, u32[]{:S(2)}) copy-start(f32[1,8,4,2,360]{4,1,3,2,0:T(8,128)} %copy-done.25) | copy-start | bytes 276484
  832.5 179.0 %copy-start.41 = (f32[1,8,4,2,360]{4,1,3,2,0:T(8,128)S(1)}, f32[1,8,4,2,360]{4,1,3,2,0:T(8,128)}, u32[]{:S(2)}) copy-start(f32[1,8,4,2,360]{4,1,3,2,0:T(8,128)} %fusion.131) | copy-start | bytes 276484
  1000.0 10.3 collective-permute-start.14
  1001.3 9.0 collective-permute-start.15
  1004.3 6.0 collective-permute-start.6
  1005.6 4.7 collective-permute-start.7
  1023.6 120.2 %all-to-all-start.7 = ((bf16[3,64,360]{2,0,1:T(4,128)(2,1)}), bf16[3,64,360]{2,0,1:T(4,128)(2,1)S(1)}, u32[]{:S(2)}, u32[]{:S(2)}) async-start(bf16[3,64,360]{2,0,1:T(4,128)(2,1)} %copy.371), calls=%async_computation.7 | async-start | bytes 393216 | tf_op jit(solution)/shard_map/all_to_all | solution.py:102
  1028.3 485.1 %all-reduce.6.cloned.1.call-start = ((), (), s32[]{:S(2)}) async-start(), calls=%async_computation.8 | async-start | bytes 2359296 | tf_op jit(solution)/shard_map/psum | solution.py:187
  (51 other events, 772.1 us)
Sparse Core Ops, SparseCore 0:
  832.8 161.0 all-reduce.7
Sparse Core Ops, SparseCore 1:
  1036.0 477.4 all-reduce.5
where the time goes:
time: 1530 us
  blocking collectives  694 us (45%)
  waiting for transfers between devices  552 us (36%)
  starting transfers between devices  121 us (8%)
  local copies, waits for them, and re-layouts  89.9 us (6%)
  other arithmetic  30.7 us (2%)
  matrix products  20.7 us (1%)
  between operations  16.9 us (1%)
    all_gather x8, blocking collectives, carried_in(): gathered = jax.tree.map(lambda a: lax.all_gather(a, axis), part)  504 us
    psum x1, waiting for transfers between devices, on_device(): lax.psum((local_grads[0], local_grads[1], local_grads[2], local_grads[3])...  369 us
    psum x1, waiting for transfers between devices, vertical_sums(): lax.psum((rising_part, falling_part), ('lev', 'sec'))  161 us
    psum x1, blocking collectives, on_device(): lax.psum((local_grads[0], local_grads[1], local_grads[2], local_grads[3])...  112 us
    psum x1, blocking collectives, vertical_sums(): lax.psum((rising_part, falling_part), ('lev', 'sec'))  78.4 us
    all_to_all x4, starting transfers between devices, to_columns(): lax.all_to_all(flattened, ('lev', 'sec'), split_axis=2, concat_axis=1, ti...  45.6 us
    all_to_all x4, starting transfers between devices, to_levels(): lax.all_to_all(regrouped, ('lev', 'sec'), split_axis=1, concat_axis=2, ti...  37.3 us
    unnamed x164, local copies, waits for them, and re-layouts  35 us
  transfers between devices with their start and end apart: 26, of which 5 were waited for; matrix products, arithmetic and copies ran while one was open for 7% of the time, Pallas kernels for 0%

commit v1 on v0

--- a/solution.py
+++ b/solution.py
@@ -66,7 +66,7 @@
     before, falling_before = carried_in(
         (rising_part, falling_part), ("lev", "sec"), add_pairs, (zeros_part, zeros_part)
     )
-    column_sum, falling_total = lax.psum((rising_part, falling_part), ("lev", "sec"))
+    column_sum, falling_total = lax.psum(lax.psum((rising_part, falling_part), "sec"), "lev")
     beyond = falling_total - falling_before - falling_part
     return (before + rising_run, beyond + falling_run, column_sum)
 

time: 1530 us -> 1460 us (0.954)
  waiting for transfers between devices: 552 us -> 508 us
  blocking collectives: 694 us -> 658 us
    psum x1 -> x2, waiting for transfers between devices: 161 us -> 115 us  [the longest x1 65.4 us: vertical_sums(): lax.psum((rising_part, falling_part), 'sec')]
    psum x1 -> x2, blocking collectives: 78.4 us -> 42.4 us  [the longest x1 25.7 us: vertical_sums(): lax.psum((rising_part, falling_part), 'sec')]
  transfers between devices with their start and end apart: 26 -> 27, of which waited for: 5 -> 6; matrix products, arithmetic and copies ran while one was open for 7% -> 7% of each run, Pallas kernels for 0% -> 0%
where the time goes in v1:
time: 1460 us
  blocking collectives  658 us (45%)
  waiting for transfers between devices  508 us (35%)
  starting transfers between devices  133 us (9%)
  local copies, waits for them, and re-layouts  89.9 us (6%)
  other arithmetic  30.6 us (2%)
  matrix products  20.7 us (1%)
  between operations  16.9 us (1%)
    all_gather x8, blocking collectives, carried_in(): gathered = jax.tree.map(lambda a: lax.all_gather(a, axis), part)  505 us
    psum x1, waiting for transfers between devices, on_device(): lax.psum((local_grads[0], local_grads[1], local_grads[2], local_grads[3])...  370 us
    psum x1, blocking collectives, on_device(): lax.psum((local_grads[0], local_grads[1], local_grads[2], local_grads[3])...  110 us
    psum x1, waiting for transfers between devices, vertical_sums(): lax.psum((rising_part, falling_part), 'sec')  65.4 us
    psum x1, waiting for transfers between devices, vertical_sums(): lax.psum(lax.psum((rising_part, falling_part), 'sec'), 'lev')  49.4 us
    all_to_all x4, starting transfers between devices, to_levels(): lax.all_to_all(regrouped, ('lev', 'sec'), split_axis=1, concat_axis=2, ti...  48.6 us
    all_to_all x4, starting transfers between devices, to_columns(): lax.all_to_all(flattened, ('lev', 'sec'), split_axis=2, concat_axis=1, ti...  45.7 us
    unnamed x164, local copies, waits for them, and re-layouts  35 us
  transfers between devices with their start and end apart: 27, of which 6 were waited for; matrix products, arithmetic and copies ran while one was open for 7% of the time, Pallas kernels for 0%

profile of v1, /device:TPU:8, one launch (start us, length us, event | category | flops | bytes accessed | tf_op | source)
XLA Modules:
  0.0 1456.5 jit_solution(16353696551025910852)
XLA Ops:
  11.7 3.6 collective-permute-start.1
  19.7 3.7 collective-permute-start.9
  25.1 4.8 copy.305
  30.0 2.8 reshape.435
  32.7 18.2 %all-to-all-start = ((bf16[8,2,4320]{2,1,0:T(2,128)(2,1)}), bf16[8,2,4320]{2,1,0:T(2,128)(2,1)}, u32[]{:S(2)}, u32[]{:S(2)}) async-start(bf16[8,2,4320]{2,1,0:T(2,128)(2,1)} %reshape.435), calls=%async_computation | async-start | bytes 278528 | tf_op jit(solution)/shard_map/all_to_all | solution.py:97
  62.3 63.0 %all_gather.29 = f32[8,4,2,360]{3,1,2,0:T(4,128)} all-gather(f32[1,4,2,360]{3,1,2,0:T(4,128)S(1)} %copy.336), channel_id=1, replica_groups=mesh['lev'=4,'tile'=64,'sec'=2] {'lev','sec'}, dimensions={0}, use_global_device_ids=true | all-gather | bytes 103680 | tf_op jit(solution)/shard_map/all_gather | solution.py:30
  125.9 25.7 %all-reduce.4 = (f32[4,2,360]{2,1,0:T(2,128)S(1)}, f32[4,2,360]{2,1,0:T(2,128)S(1)}) all-reduce(f32[4,2,360]{2,1,0:T(2,128)S(1)} %get-tuple-element.436, f32[4,2,360]{2,1,0:T(2,128)S(1)} %get-tuple-element.461), channel_id=1, replica_groups=mesh['lev'=4,'tile'=64,'sec'=2] {'sec'}, use_global_device_ids=true, to_apply=%region_1.2 | all-reduce | flops 5760 | bytes 46080 | tf_op jit(solution)/shard_map/psum | solution.py:69
  151.5 16.7 %all-reduce.2 = (f32[4,2,360]{2,1,0:T(2,128)}, f32[4,2,360]{2,1,0:T(2,128)}) all-reduce(f32[4,2,360]{2,1,0:T(2,128)S(1)} %get-tuple-element.353, f32[4,2,360]{2,1,0:T(2,128)S(1)} %get-tuple-element.354), channel_id=1, replica_groups=mesh['lev'=4,'tile'=64,'sec'=2] {'lev'}, use_global_device_ids=true, to_apply=%region_2.3 | all-reduce | flops 5760 | bytes 46080 | tf_op jit(solution)/shard_map/psum | solution.py:69
  168.3 2.7 copy.380
  171.0 2.8 reshape.439
  173.8 64.2 %all_gather.25 = f32[8,4,2,360]{3,1,2,0:T(4,128)S(1)} all-gather(f32[1,4,2,360]{3,1,2,0:T(4,128)S(1)} %copy.295), channel_id=1, replica_groups=mesh['lev'=4,'tile'=64,'sec'=2] {'lev','sec'}, dimensions={0}, use_global_device_ids=true | all-gather | bytes 103680 | tf_op jit(solution)/shard_map/all_gather | solution.py:30
  240.1 62.9 %all_gather.24 = f32[8,4,2,360]{3,1,2,0:T(4,128)S(1)} all-gather(f32[1,4,2,360]{3,1,2,0:T(4,128)S(1)} %copy.294), channel_id=1, replica_groups=mesh['lev'=4,'tile'=64,'sec'=2] {'lev','sec'}, dimensions={0}, use_global_device_ids=true | all-gather | bytes 103680 | tf_op jit(solution)/shard_map/all_gather | solution.py:30
  308.4 63.0 %all_gather.28 = f32[8,4,2,360]{3,1,2,0:T(4,128)S(1)} all-gather(f32[1,4,2,360]{3,1,2,0:T(4,128)S(1)} %copy.335), channel_id=1, replica_groups=mesh['lev'=4,'tile'=64,'sec'=2] {'lev','sec'}, dimensions={0}, use_global_device_ids=true | all-gather | bytes 103680 | tf_op jit(solution)/shard_map/all_gather | solution.py:30
  376.4 3.6 collective-permute-start.3
  381.9 3.6 collective-permute-start.11
  387.7 8.6 all-to-all-start.4
  396.3 3.0 reshape.436
  399.3 2.2 copy.376
  401.5 3.2 fusion.23
  408.0 2.3 all-to-all-done.4
  410.3 12.3 all-to-all-start.1
  426.9 3.0 reshape.440
  429.9 2.2 copy.382
  432.2 10.0 all-to-all-done.1
  449.5 3.0 collective-permute-start.5
  453.1 2.7 copy.377
  455.8 2.8 reshape.437
  458.6 4.4 all-to-all-start.2
  463.0 62.2 %all_gather.27 = f32[8,4,2,360]{3,1,2,0:T(4,128)S(1)} all-gather(f32[1,4,2,360]{3,1,2,0:T(4,128)S(1)} %copy.318), channel_id=1, replica_groups=mesh['lev'=4,'tile'=64,'sec'=2] {'lev','sec'}, dimensions={0}, use_global_device_ids=true | all-gather | bytes 103680 | tf_op jit(solution)/shard_map/all_gather | solution.py:30
  527.8 63.5 %all_gather.26 = f32[8,4,2,360]{3,1,2,0:T(4,128)S(1)} all-gather(f32[1,4,2,360]{3,1,2,0:T(4,128)S(1)} %copy.317), channel_id=1, replica_groups=mesh['lev'=4,'tile'=64,'sec'=2] {'lev','sec'}, dimensions={0}, use_global_device_ids=true | all-gather | bytes 103680 | tf_op jit(solution)/shard_map/all_gather | solution.py:30
  592.3 3.0 reshape.438
  602.9 15.5 %all-to-all-start.5 = ((bf16[3,64,360]{2,0,1:T(4,128)(2,1)}), bf16[3,64,360]{2,0,1:T(4,128)(2,1)S(1)}, u32[]{:S(2)}, u32[]{:S(2)}) async-start(bf16[3,64,360]{2,0,1:T(4,128)(2,1)} %copy.349), calls=%async_computation.5 | async-start | bytes 393216 | tf_op jit(solution)/shard_map/all_to_all | solution.py:102
  621.6 10.7 all-to-all-done.5
  632.3 6.0 all-to-all-start.3
  643.3 3.6 collective-permute-start.13
  646.9 2.7 copy.383
  649.7 2.8 reshape.441
  654.6 14.6 all-to-all-start.6
  670.7 62.6 %all_gather.31 = f32[8,4,2,360]{3,1,2,0:T(4,128)S(1)} all-gather(f32[1,4,2,360]{3,1,2,0:T(4,128)S(1)} %copy.357), channel_id=1, replica_groups=mesh['lev'=4,'tile'=64,'sec'=2] {'lev','sec'}, dimensions={0}, use_global_device_ids=true | all-gather | bytes 103680 | tf_op jit(solution)/shard_map/all_gather | solution.py:30
  735.4 63.5 %all_gather.30 = f32[8,4,2,360]{3,1,2,0:T(4,128)S(1)} all-gather(f32[1,4,2,360]{3,1,2,0:T(4,128)S(1)} %copy.356), channel_id=1, replica_groups=mesh['lev'=4,'tile'=64,'sec'=2] {'lev','sec'}, dimensions={0}, use_global_device_ids=true | all-gather | bytes 103680 | tf_op jit(solution)/shard_map/all_gather | solution.py:30
  799.3 65.4 %all-reduce.13.cloned.1.call-done = (f32[4,2,360]{2,1,0:T(2,128)}, f32[4,2,360]{2,1,0:T(2,128)}, f32[4,2,360]{2,1,0:T(2,128)}, f32[4,2,360]{2,1,0:T(2,128)}, f32[4,2,360]{2,1,0:T(2,128)}, /*index=5*/f32[4,2,360]{2,1,0:T(2,128)}) async-done(((f32[4,2,360]{2,1,0:T(2,128)}, f32[4,2,360]{2,1,0:T(2,128)}, f32[4,2,360]{2,1,0:T(2,128)}, f32[4,2,360]{2,1,0:T(2,128)}, f32[4,2,360]{2,1,0:T(2,128)}, ...) | async-done | bytes 69136 | tf_op jit(solution)/shard_map/psum | solution.py:69
  865.4 49.4 %all-reduce.11.cloned.1.call-done = (f32[4,2,360]{2,1,0:T(2,128)}, f32[4,2,360]{2,1,0:T(2,128)}, f32[4,2,360]{2,1,0:T(2,128)}, f32[4,2,360]{2,1,0:T(2,128)}, f32[4,2,360]{2,1,0:T(2,128)}, /*index=5*/f32[4,2,360]{2,1,0:T(2,128)}) async-done(((f32[4,2,360]{2,1,0:T(2,128)}, f32[4,2,360]{2,1,0:T(2,128)}, f32[4,2,360]{2,1,0:T(2,128)}, f32[4,2,360]{2,1,0:T(2,128)}, f32[4,2,360]{2,1,0:T(2,128)}, ...) | async-done | bytes 69136 | tf_op jit(solution)/shard_map/psum | solution.py:69
  922.0 3.0 collective-permute-start.15
  926.4 3.5 collective-permute-start.7
  933.2 3.0 reshape.442
  944.4 14.9 %all-to-all-start.7 = ((bf16[3,64,360]{2,0,1:T(4,128)(2,1)}), bf16[3,64,360]{2,0,1:T(4,128)(2,1)S(1)}, u32[]{:S(2)}, u32[]{:S(2)}) async-start(bf16[3,64,360]{2,0,1:T(4,128)(2,1)} %copy.371), calls=%async_computation.7 | async-start | bytes 393216 | tf_op jit(solution)/shard_map/all_to_all | solution.py:102
  962.5 110.5 %psum.195 = f32[2,384]{1,0:T(2,128)} all-reduce(f32[2,384]{1,0:T(2,128)S(1)} %maximum_add_fusion.2), channel_id=1, replica_groups=mesh['lev'=4,'tile'=64,'sec'=2] {'lev','tile','sec'}, use_global_device_ids=true, to_apply=%region_40.41 | all-reduce | flops 768 | bytes 6144 | tf_op jit(solution)/shard_map/psum | solution.py:187
  1073.9 369.9 %all-reduce.9.cloned.1.call-done = (f32[192,384]{1,0:T(8,128)}, f32[384,384]{1,0:T(8,128)}, f32[384,192]{0,1:T(8,128)}) async-done(((f32[192,384]{1,0:T(8,128)}, f32[384,384]{1,0:T(8,128)}, f32[384,192]{0,1:T(8,128)}), (f32[192,384]{1,0:T(8,128)}, f32[384,384]{1,0:T(8,128)}, f32[384,192]{0,1:T(8,128)})) %all-reduce.9.cloned.1.call-update) | async-done | bytes 1179664 | tf_op jit(solution)/shard_map/psum | solution.py:187
  (375 shorter events, 110.1 us)
Async XLA Ops:
  8.0 396.7 %copy-start = (bf16[384,384]{1,0:T(8,128)(2,1)S(1)}, bf16[384,384]{1,0:T(8,128)(2,1)}, u32[]{:S(2)}) copy-start(bf16[384,384]{1,0:T(8,128)(2,1)} %param.23) | copy-start | bytes 884740
  10.4 227.6 %collective-permute-start = (f32[8,4,1,360]{3,2,1,0:T(1,128)}, f32[8,4,1,360]{3,2,1,0:T(1,128)}, u32[]{:S(2)}, u32[]{:S(2)}) collective-permute-start(f32[8,4,1,360]{3,2,1,0:T(1,128)} %get-tuple-element.442), channel_id=1, source_target_pairs={{2,0},{4,2},{6,4},{8,6},{10,8},{12,10},{14,12},{16,14},{18,16},{20... | collective-permute-start | bytes 138248 | tf_op jit(solution)/shard_map/ppermute | solution.py:23
  11.7 226.3 %collective-permute-start.1 = (f32[8,4,1,360]{3,2,1,0:T(1,128)}, f32[8,4,1,360]{3,2,1,0:T(1,128)}, u32[]{:S(2)}, u32[]{:S(2)}) collective-permute-start(f32[8,4,1,360]{3,2,1,0:T(1,128)} %get-tuple-element.443), channel_id=1, source_target_pairs={{0,2},{2,4},{4,6},{6,8},{8,10},{10,12},{12,14},{14,16},{16,18},{18... | collective-permute-start | bytes 138248 | tf_op jit(solution)/shard_map/ppermute | solution.py:22
  18.4 288.2 %collective-permute-start.8 = (f32[8,4,1,360]{3,2,1,0:T(1,128)}, f32[8,4,1,360]{3,2,1,0:T(1,128)}, u32[]{:S(2)}, u32[]{:S(2)}) collective-permute-start(f32[8,4,1,360]{3,2,1,0:T(1,128)} %get-tuple-element.416), channel_id=1, source_target_pairs={{2,0},{4,2},{6,4},{8,6},{10,8},{12,10},{14,12},{16,14},{18,16},{20... | collective-permute-start | bytes 138248 | tf_op jit(solution)/shard_map/ppermute | solution.py:23
  19.7 286.9 %collective-permute-start.9 = (f32[8,4,1,360]{3,2,1,0:T(1,128)}, f32[8,4,1,360]{3,2,1,0:T(1,128)}, u32[]{:S(2)}, u32[]{:S(2)}) collective-permute-start(f32[8,4,1,360]{3,2,1,0:T(1,128)} %get-tuple-element.417), channel_id=1, source_target_pairs={{0,2},{2,4},{4,6},{6,8},{8,10},{10,12},{12,14},{14,16},{16,18},{18... | collective-permute-start | bytes 138248 | tf_op jit(solution)/shard_map/ppermute | solution.py:22
  32.7 355.0 %all-to-all-start = ((bf16[8,2,4320]{2,1,0:T(2,128)(2,1)}), bf16[8,2,4320]{2,1,0:T(2,128)(2,1)}, u32[]{:S(2)}, u32[]{:S(2)}) async-start(bf16[8,2,4320]{2,1,0:T(2,128)(2,1)} %reshape.435), calls=%async_computation | async-start | bytes 278528 | tf_op jit(solution)/shard_map/all_to_all | solution.py:97
  173.8 132.9 %copy-start.20 = (f32[8,4,2,360]{3,2,1,0:T(2,128)S(1)}, f32[8,4,2,360]{3,2,1,0:T(2,128)}, u32[]{:S(2)}) copy-start(f32[8,4,2,360]{3,2,1,0:T(2,128)} %copy-done.19) | copy-start | bytes 276484
  173.8 132.9 %copy-start.43 = (f32[8,4,2,359]{3,2,1,0:T(2,128)S(1)}, f32[8,4,2,359]{3,2,1,0:T(2,128)}, u32[]{:S(2)}) copy-start(f32[8,4,2,359]{3,2,1,0:T(2,128)} %get-tuple-element.414) | copy-start | bytes 275716
  173.8 132.9 %copy-start.44 = (f32[8,4,2,359]{3,2,1,0:T(2,128)S(1)}, f32[8,4,2,359]{3,2,1,0:T(2,128)}, u32[]{:S(2)}) copy-start(f32[8,4,2,359]{3,2,1,0:T(2,128)} %get-tuple-element.415) | copy-start | bytes 275716
  173.8 132.9 %copy-start.54 = (f32[8,4,2,1]{3,2,1,0:T(2,128)S(1)}, f32[8,4,2,1]{3,2,1,0:T(2,128)}, u32[]{:S(2)}) copy-start(f32[8,4,2,1]{3,2,1,0:T(2,128)} %get-tuple-element.412) | copy-start | bytes 772
  173.8 132.9 %copy-start.55 = (f32[8,4,2,1]{3,2,1,0:T(2,128)S(1)}, f32[8,4,2,1]{3,2,1,0:T(2,128)}, u32[]{:S(2)}) copy-start(f32[8,4,2,1]{3,2,1,0:T(2,128)} %get-tuple-element.413) | copy-start | bytes 772
  173.8 199.2 %copy-start.65 = (f32[8]{0:T(128)S(1)}, f32[8]{0:T(128)}, u32[]{:S(2)}) copy-start(f32[8]{0:T(128)} %copy-done.64) | copy-start | bytes 100
  173.8 199.9 %copy-start.39 = (f32[8,4,2,360]{3,2,1,0:T(2,128)S(1)}, f32[8,4,2,360]{3,2,1,0:T(2,128)}, u32[]{:S(2)}) copy-start(f32[8,4,2,360]{3,2,1,0:T(2,128)} %copy-done.38) | copy-start | bytes 276484
  173.8 199.9 %copy-start.63 = (f32[4,2,360]{2,1,0:T(2,128)S(1)}, f32[4,2,360]{2,1,0:T(2,128)}, u32[]{:S(2)}) copy-start(f32[4,2,360]{2,1,0:T(2,128)} %get-tuple-element.346) | copy-start | bytes 34564
  173.8 199.9 %copy-start.58 = (f32[4,2,360]{2,1,0:T(2,128)S(1)}, f32[4,2,360]{2,1,0:T(2,128)}, u32[]{:S(2)}) copy-start(f32[4,2,360]{2,1,0:T(2,128)} %param.20) | copy-start | bytes 34564
  238.0 147.7 %copy-start.61 = (f32[2]{0:T(128)S(1)}, f32[2]{0:T(128)}, u32[]{:S(2)}) copy-start(f32[2]{0:T(128)} %fusion.149) | copy-start | bytes 28
  375.1 48.8 %collective-permute-start.2 = (f32[8,4,1,360]{3,2,1,0:T(1,128)}, f32[8,4,1,360]{3,2,1,0:T(1,128)}, u32[]{:S(2)}, u32[]{:S(2)}) collective-permute-start(f32[8,4,1,360]{3,2,1,0:T(1,128)} %get-tuple-element.434), channel_id=1, source_target_pairs={{2,0},{4,2},{6,4},{8,6},{10,8},{12,10},{14,12},{16,14},{18,16},{20... | collective-permute-start | bytes 138248 | tf_op jit(solution)/shard_map/ppermute | solution.py:23
  376.4 47.5 %collective-permute-start.3 = (f32[8,4,1,360]{3,2,1,0:T(1,128)}, f32[8,4,1,360]{3,2,1,0:T(1,128)}, u32[]{:S(2)}, u32[]{:S(2)}) collective-permute-start(f32[8,4,1,360]{3,2,1,0:T(1,128)} %get-tuple-element.435), channel_id=1, source_target_pairs={{0,2},{2,4},{4,6},{6,8},{8,10},{10,12},{12,14},{14,16},{16,18},{18... | collective-permute-start | bytes 138248 | tf_op jit(solution)/shard_map/ppermute | solution.py:22
  380.6 43.3 %collective-permute-start.10 = (f32[8,4,1,360]{3,2,1,0:T(1,128)}, f32[8,4,1,360]{3,2,1,0:T(1,128)}, u32[]{:S(2)}, u32[]{:S(2)}) collective-permute-start(f32[8,4,1,360]{3,2,1,0:T(1,128)} %get-tuple-element.406), channel_id=1, source_target_pairs={{2,0},{4,2},{6,4},{8,6},{10,8},{12,10},{14,12},{16,14},{18,16},{20... | collective-permute-start | bytes 138248 | tf_op jit(solution)/shard_map/ppermute | solution.py:23
  381.9 42.0 %collective-permute-start.11 = (f32[8,4,1,360]{3,2,1,0:T(1,128)}, f32[8,4,1,360]{3,2,1,0:T(1,128)}, u32[]{:S(2)}, u32[]{:S(2)}) collective-permute-start(f32[8,4,1,360]{3,2,1,0:T(1,128)} %get-tuple-element.407), channel_id=1, source_target_pairs={{0,2},{2,4},{4,6},{6,8},{8,10},{10,12},{12,14},{14,16},{16,18},{18... | collective-permute-start | bytes 138248 | tf_op jit(solution)/shard_map/ppermute | solution.py:22
  387.7 22.6 %all-to-all-start.4 = ((bf16[8,2,4320]{2,1,0:T(2,128)(2,1)}), bf16[8,2,4320]{2,1,0:T(2,128)(2,1)}, u32[]{:S(2)}, u32[]{:S(2)}) async-start(bf16[8,2,4320]{2,1,0:T(2,128)(2,1)} %reshape.439), calls=%async_computation.4 | async-start | bytes 278528 | tf_op jit(solution)/shard_map/all_to_all | solution.py:97
  410.3 31.8 %all-to-all-start.1 = ((bf16[3,64,360]{2,0,1:T(4,128)(2,1)}), bf16[3,64,360]{2,0,1:T(4,128)(2,1)}, u32[]{:S(2)}, u32[]{:S(2)}) async-start(bf16[3,64,360]{2,0,1:T(4,128)(2,1)} %copy.308), calls=%async_computation.1 | async-start | bytes 393216 | tf_op jit(solution)/shard_map/all_to_all | solution.py:102
  448.2 77.1 %collective-permute-start.4 = (f32[8,4,1,360]{3,2,1,0:T(1,128)}, f32[8,4,1,360]{3,2,1,0:T(1,128)S(1)}, u32[]{:S(2)}, u32[]{:S(2)}) collective-permute-start(f32[8,4,1,360]{3,2,1,0:T(1,128)} %get-tuple-element.428), channel_id=1, source_target_pairs={{2,0},{4,2},{6,4},{8,6},{10,8},{12,10},{14,12},{16,14},{18,16},{20... | collective-permute-start | bytes 138248 | tf_op jit(solution)/shard_map/ppermute | solution.py:23
  449.5 75.8 %collective-permute-start.5 = (f32[8,4,1,360]{3,2,1,0:T(1,128)}, f32[8,4,1,360]{3,2,1,0:T(1,128)S(1)}, u32[]{:S(2)}, u32[]{:S(2)}) collective-permute-start(f32[8,4,1,360]{3,2,1,0:T(1,128)} %get-tuple-element.429), channel_id=1, source_target_pairs={{0,2},{2,4},{4,6},{6,8},{8,10},{10,12},{12,14},{14,16},{16,18},{18... | collective-permute-start | bytes 138248 | tf_op jit(solution)/shard_map/ppermute | solution.py:22
  458.6 133.7 %all-to-all-start.2 = ((bf16[8,2,4320]{2,1,0:T(2,128)(2,1)}), bf16[8,2,4320]{2,1,0:T(2,128)(2,1)}, u32[]{:S(2)}, u32[]{:S(2)}) async-start(bf16[8,2,4320]{2,1,0:T(2,128)(2,1)} %reshape.437), calls=%async_computation.2 | async-start | bytes 278528 | tf_op jit(solution)/shard_map/all_to_all | solution.py:97
  602.9 29.5 %all-to-all-start.5 = ((bf16[3,64,360]{2,0,1:T(4,128)(2,1)}), bf16[3,64,360]{2,0,1:T(4,128)(2,1)S(1)}, u32[]{:S(2)}, u32[]{:S(2)}) async-start(bf16[3,64,360]{2,0,1:T(4,128)(2,1)} %copy.349), calls=%async_computation.5 | async-start | bytes 393216 | tf_op jit(solution)/shard_map/all_to_all | solution.py:102
  632.3 22.2 %all-to-all-start.3 = ((bf16[3,64,360]{2,0,1:T(4,128)(2,1)}), bf16[3,64,360]{2,0,1:T(4,128)(2,1)}, u32[]{:S(2)}, u32[]{:S(2)}) async-start(bf16[3,64,360]{2,0,1:T(4,128)(2,1)} %copy.333), calls=%async_computation.3 | async-start | bytes 393216 | tf_op jit(solution)/shard_map/all_to_all | solution.py:102
  642.0 91.3 %collective-permute-start.12 = (f32[8,4,1,360]{3,2,1,0:T(1,128)}, f32[8,4,1,360]{3,2,1,0:T(1,128)}, u32[]{:S(2)}, u32[]{:S(2)}) collective-permute-start(f32[8,4,1,360]{3,2,1,0:T(1,128)} %get-tuple-element.400), channel_id=1, source_target_pairs={{2,0},{4,2},{6,4},{8,6},{10,8},{12,10},{14,12},{16,14},{18,16},{20... | collective-permute-start | bytes 138248 | tf_op jit(solution)/shard_map/ppermute | solution.py:23
  643.3 90.1 %collective-permute-start.13 = (f32[8,4,1,360]{3,2,1,0:T(1,128)}, f32[8,4,1,360]{3,2,1,0:T(1,128)}, u32[]{:S(2)}, u32[]{:S(2)}) collective-permute-start(f32[8,4,1,360]{3,2,1,0:T(1,128)} %get-tuple-element.401), channel_id=1, source_target_pairs={{0,2},{2,4},{4,6},{6,8},{8,10},{10,12},{12,14},{14,16},{16,18},{18... | collective-permute-start | bytes 138248 | tf_op jit(solution)/shard_map/ppermute | solution.py:22
  652.4 212.2 %copy-start.67 = (f32[8]{0:T(128)S(1)}, f32[8]{0:T(128)}, u32[]{:S(2)}) copy-start(f32[8]{0:T(128)} %copy-done.64) | copy-start | bytes 100
  652.4 262.3 %copy-start.59 = (f32[4,2,360]{2,1,0:T(2,128)S(1)}, f32[4,2,360]{2,1,0:T(2,128)}, u32[]{:S(2)}) copy-start(f32[4,2,360]{2,1,0:T(2,128)} %param.20) | copy-start | bytes 34564
  652.4 264.6 %copy-start.37 = (f32[8,4,2,360]{3,2,1,0:T(2,128)S(1)}, f32[8,4,2,360]{3,2,1,0:T(2,128)}, u32[]{:S(2)}) copy-start(f32[8,4,2,360]{3,2,1,0:T(2,128)} %copy-done.36) | copy-start | bytes 276484
  652.4 265.3 %copy-start.60 = (f32[4,2,360]{2,1,0:T(2,128)S(1)}, f32[4,2,360]{2,1,0:T(2,128)}, u32[]{:S(2)}) copy-start(f32[4,2,360]{2,1,0:T(2,128)} %param.18) | copy-start | bytes 34564
  654.5 275.4 %copy-start.18 = (f32[1,8,4,2,360]{4,1,3,2,0:T(8,128)S(1)}, f32[1,8,4,2,360]{4,1,3,2,0:T(8,128)}, u32[]{:S(2)}) copy-start(f32[1,8,4,2,360]{4,1,3,2,0:T(8,128)} %copy-done.17) | copy-start | bytes 276484
  654.5 275.4 %copy-start.62 = (f32[2]{0:T(128)S(1)}, f32[2]{0:T(128)}, u32[]{:S(2)}) copy-start(f32[2]{0:T(128)} %fusion.149) | copy-start | bytes 28
  654.6 278.6 %all-to-all-start.6 = ((bf16[8,2,4320]{2,1,0:T(2,128)(2,1)}), bf16[8,2,4320]{2,1,0:T(2,128)(2,1)}, u32[]{:S(2)}, u32[]{:S(2)}) async-start(bf16[8,2,4320]{2,1,0:T(2,128)(2,1)} %reshape.441), calls=%async_computation.6 | async-start | bytes 278528 | tf_op jit(solution)/shard_map/all_to_all | solution.py:97
  669.1 195.5 %all-reduce.13.cloned.1.call-start = ((), (), s32[]{:S(2)}) async-start(), calls=%async_computation.10 | async-start | bytes 147456 | tf_op jit(solution)/shard_map/psum | solution.py:69
  670.1 260.2 %copy-start.4 = (f32[3,8,4,2,360]{4,1,3,2,0:T(8,128)S(1)}, f32[3,8,4,2,360]{4,1,3,2,0:T(8,128)}, u32[]{:S(2)}) copy-start(f32[3,8,4,2,360]{4,1,3,2,0:T(8,128)} %copy-done.3) | copy-start | bytes 829444
  734.7 196.4 %copy-start.24 = (f32[1,8,4,2,360]{4,1,3,2,0:T(8,128)S(1)}, f32[1,8,4,2,360]{4,1,3,2,0:T(8,128)}, u32[]{:S(2)}) copy-start(f32[1,8,4,2,360]{4,1,3,2,0:T(8,128)} %copy-done.23) | copy-start | bytes 276484
  734.7 196.4 %copy-start.26 = (f32[1,8,4,2,360]{4,1,3,2,0:T(8,128)S(1)}, f32[1,8,4,2,360]{4,1,3,2,0:T(8,128)}, u32[]{:S(2)}) copy-start(f32[1,8,4,2,360]{4,1,3,2,0:T(8,128)} %copy-done.25) | copy-start | bytes 276484
  799.0 115.7 %all-reduce.11.cloned.1.call-start = ((), (), s32[]{:S(2)}) async-start(), calls=%async_computation.9 | async-start | bytes 147456 | tf_op jit(solution)/shard_map/psum | solution.py:69
  799.1 133.2 %copy-start.41 = (f32[1,8,4,2,360]{4,1,3,2,0:T(8,128)S(1)}, f32[1,8,4,2,360]{4,1,3,2,0:T(8,128)}, u32[]{:S(2)}) copy-start(f32[1,8,4,2,360]{4,1,3,2,0:T(8,128)} %fusion.131) | copy-start | bytes 276484
  920.7 10.3 collective-permute-start.14
  922.0 9.0 collective-permute-start.15
  925.1 6.0 collective-permute-start.6
  926.4 4.7 collective-permute-start.7
  944.4 128.5 %all-to-all-start.7 = ((bf16[3,64,360]{2,0,1:T(4,128)(2,1)}), bf16[3,64,360]{2,0,1:T(4,128)(2,1)S(1)}, u32[]{:S(2)}, u32[]{:S(2)}) async-start(bf16[3,64,360]{2,0,1:T(4,128)(2,1)} %copy.371), calls=%async_computation.7 | async-start | bytes 393216 | tf_op jit(solution)/shard_map/all_to_all | solution.py:102
  959.3 484.5 %all-reduce.9.cloned.1.call-start = ((), (), s32[]{:S(2)}) async-start(), calls=%async_computation.8 | async-start | bytes 2359296 | tf_op jit(solution)/shard_map/psum | solution.py:187
  (52 other events, 947.9 us)
Sparse Core Ops, SparseCore 0:
  799.1 65.4 all-reduce.12
  867.4 47.3 all-reduce.10
Sparse Core Ops, SparseCore 1:
  966.9 476.8 all-reduce.8
